TPU v7x, 256 devices: a whole 4x4x8 slice. The times are simulated.
256 devices in a mesh: dp: 16 (over x, y), tensor: 16 (over z, core).
Axes of the slice: x: 4, y: 4, z: 8, core: 2. Of those that a mesh axis runs over, the one named last changes fastest.
Arguments:
- activations: bfloat16 [32, 256, 8192], P('dp', None, 'tensor'), may hold values from -16 to 16
- out_grads: bfloat16 [32, 256, 8192], P('dp', None, 'tensor'), may hold values from -8 to 8
- lengths: int32 [32], P('dp'), may hold values from 64 to 256, as said below
Outputs:
- grad_weight: bfloat16 [8192, 8192], P('dp', 'tensor')
- seq_norms: float32 [32], P('dp')
Inputs may be any that keep to these rules, and one draw needn't show every extreme that they name: `lengths`: every sequence has at least 64 live positions; some sequence has exactly 256 and some exactly 64 in every draw.
All inputs are finite; a program needn't handle non-finite values.
Results may differ from a plain program's by a relative error of at most 0.019.
Values may be sent and summed in bfloat16 or wider, within the bound.
A program may use at most 192 MiB of HBM per device.

v0:
```python
import math

import jax
import jax.numpy as jnp
from jax import lax
from jax.experimental import pallas as pl
from jax.experimental.pallas import tpu as pltpu
from jax.sharding import PartitionSpec as P

D = 8192
K = 8192
SLOT_LEN = 256
SEQS = 32
X, Y, Z = 4, 4, 8
NQ = 2
W = 256
F = 512
BOUND = math.sqrt(K * D * SLOT_LEN / 2.0)
F32 = jnp.float32
BF16 = jnp.bfloat16

FIRST = (
    ("pairs",), ("yl",), ("yf", 0),
)
SOURCE = (
    ("o", 0), ("pairw",), ("ring", 1), ("yf", 1), ("ring", 2), ("o", 1), ("ring", 3), ("acts", 3),
    ("acts", 1), ("ring", 4), ("o", 2), ("ringend",), ("szs",), ("o", 3), ("r", 1, 2, 0), ("r", 0, 2, 0),
    ("arel", 0), ("arel", 1), ("szw",), ("r", 0, 2, 1), ("r", 1, 2, 1), ("syw",), ("aw",), ("r", 1, 2, 2),
    ("C",), ("r", 0, 2, 2), ("C",), ("r", 1, 2, 3), ("C",), ("r", 0, 2, 3), ("C",), ("C",), ("C",),
    ("r", 0, 4, 0), ("r", 1, 4, 1), ("r", 0, 4, 2), ("C",), ("r", 1, 4, 3), ("C",),
)
OTHER = (
    ("pairw",), ("ring", 1), ("yf", 1), ("ring", 2), ("ring", 3), ("acts", 3), ("r", 0, 1, 0), ("r", 1, 1, 0),
    ("acts", 1), ("ring", 4), ("ringend",), ("szs",), ("r", 1, 1, 1), ("r", 0, 1, 1), ("arel", 0),
    ("arel", 1), ("szw",), ("r", 1, 1, 2), ("r", 0, 1, 2), ("r", 1, 1, 3), ("r", 0, 1, 3), ("syw",), ("aw",),
    ("C",), ("r", 1, 3, 0), ("C",), ("r", 0, 3, 0), ("C",), ("C",), ("r", 1, 3, 1), ("r", 0, 3, 1),
    ("r", 1, 3, 2), ("r", 0, 3, 2), ("C",), ("r", 1, 3, 3), ("r", 0, 3, 3), ("C",), ("C",), ("C",),
)

def rcopy(src, dst, send, recv, device):
    return pltpu.make_async_remote_copy(
        src_ref=src,
        dst_ref=dst,
        send_sem=send,
        recv_sem=recv,
        device_id=device,
        device_id_type=pl.DeviceIdType.MESH,
    )


def wait_bytes(ref, sem):
    pltpu.make_async_copy(ref, ref, sem).wait()


def kernel(
    len_ref, a_hbm, g_hbm, out_ref, norm_ref,
    a_ref, g_ref, gbuf, at, ats, gpack, gpair, gsum, gup, gdn, sup, sdn, sz, sy,
    hold, own, s1, s2, s3, rl, rr, fl, fr,
    loads, ysend, yrecv, kup, kdn, zsend, zrecv, psend, precv, asend, a_up, a_dn, a_far, afsend,
    gpsend, gprecv, gupsend, guprecv, gdnsend, gdnrecv, szsend, szrecv, sysend, syrecv,
    rsend, rlrecv, rrrecv, fsend, flrecv, frrecv,
):
    dp = lax.axis_index("dp")
    tn = lax.axis_index("tensor")
    x, y = lax.div(dp, Y), lax.rem(dp, Y)
    z, c = lax.div(tn, 2), lax.rem(tn, 2)

    def dev(x_, y_, z_, c_):
        return (x_ * Y + y_, z_ * 2 + c_)

    def xs(k):
        return lax.rem(x + k, X)

    def ys(k):
        return lax.rem(y + k, Y)

    def zs(k):
        return lax.rem(z + k + Z, Z)

    partner = dev(x, y, z, 1 - c)
    z_up, z_dn = dev(x, y, zs(1), c), dev(x, y, zs(-1), c)
    x_up, x_dn = dev(xs(1), y, z, c), dev(xs(3), y, z, c)
    y_up, y_dn = dev(x, ys(1), z, c), dev(x, ys(3), z, c)
    y_others = [(ys(k), c) for k in (1, 2, 3)] + [(ys(k), 1 - c) for k in (0, 1, 2, 3)]

    load_a = pltpu.make_async_copy(a_hbm, a_ref, loads.at[0])
    load_g = pltpu.make_async_copy(g_hbm, g_ref, loads.at[1])
    load_a.start()
    load_g.start()

    barrier = pltpu.get_barrier_semaphore()
    peers = [dev(x, y2, z, c2) for y2, c2 in y_others]
    peers += [dev(x, y, zs(k), c) for k in range(1, Z)] + [x_up, x_dn]
    for peer in peers:
        pl.semaphore_signal(barrier, inc=1, device_id=peer, device_id_type=pl.DeviceIdType.MESH)
    rows = lax.broadcasted_iota(jnp.int32, (SLOT_LEN, F), 0)
    contract = (((1,), (1,)), ((), ()))
    load_a.wait()
    load_g.wait()
    for s in range(2):
        am = jnp.where(rows < len_ref[s], a_ref[s].astype(F32), 0.0)
        at[y, s] = am.T.astype(BF16)
        am = am.astype(BF16)
        g = g_ref[s]
        for m, v in enumerate((am, g)):
            full = lax.dot_general(v, v, contract, preferred_element_type=F32)
            gpack[s, :, m, 0] = full[:128, :128].reshape(Z, 16, 128)
            gpack[s, :, m, 1] = full[:128, 128:].reshape(Z, 16, 128)
            gpack[s, :, m, 2] = full[128:, 128:].reshape(Z, 16, 128)
    pl.semaphore_wait(barrier, len(peers))

    xb0 = lax.div(z, 2)
    yt = 2 * lax.rem(z, 2) + c
    is_src = lax.rem(z, 2) == lax.div(y, 2)
    steps_y = lax.rem(y - yt + Y, Y)

    def first(q, h):
        return rcopy(
            g_hbm.at[h, :, pl.ds(q * W, W)], gbuf.at[xb0, q, h, steps_y], ysend.at[q, h],
            yrecv.at[q, steps_y], dev(x, yt, z, h),
        )

    def first_steps():
        @pl.when(steps_y == 0)
        def _():
            for q in range(NQ):
                pltpu.make_async_copy(
                    g_hbm.at[c, :, pl.ds(q * W, W)], gbuf.at[xb0, q, c, 0], yrecv.at[q, 0]
                ).start()
                first(q, 1 - c).start()

        @pl.when(steps_y == 1)
        def _():
            for q in range(NQ):
                first(q, 0).start()
                first(q, 1).start()

    def first_far(q):
        @pl.when(steps_y >= 2)
        def _():
            first(q, 0).start()
            first(q, 1).start()

    pair = rcopy(gpack.at[1 - c], gpair, gpsend, gprecv, partner)

    def pair_wait():
        pair.wait_recv()
        gsum[...] = gpack[c] + gpair[...]

    def ring_up(i):
        src = gsum.at[zs(4)] if i == 1 else sup.at[i - 2]
        return rcopy(src, gup.at[i - 1], gupsend.at[i - 1], guprecv.at[i - 1], z_up)

    def ring_dn(i):
        src = gsum.at[zs(-3)] if i == 1 else sdn.at[i - 2]
        return rcopy(src, gdn.at[i - 1], gdnsend.at[i - 1], gdnrecv.at[i - 1], z_dn)

    def ring(i):
        if i > 1:
            ring_up(i - 1).wait_recv()
            sup[i - 2] = gsum[zs(5 - i)] + gup[i - 2]
        ring_up(i).start()
        if i <= 3:
            if i > 1:
                ring_dn(i - 1).wait_recv()
                sdn[i - 2] = gsum[zs(i - 4)] + gdn[i - 2]
            ring_dn(i).start()

    def ring_end():
        ring_up(4).wait_recv()
        ring_dn(3).wait_recv()
        total = gsum[z] + gup[3] + gdn[2]
        prod = total[0] * total[1]
        square = jnp.sum(prod[0] + 2.0 * prod[1] + prod[2])
        sz[z] = jnp.full((8, 128), square, F32)

    def squares():
        for k in range(1, Z):
            rcopy(sz.at[z], sz.at[z], szsend, szrecv, dev(x, y, zs(k), c)).start()

    def squares_wait():
        wait_bytes(sz.at[pl.ds(0, 7)], szrecv)
        tile = sz[0]
        for k in range(1, Z):
            tile = tile + sz[k]
        mine = y * 2 + c
        sy[mine] = tile
        for y2, c2 in y_others:
            rcopy(sy.at[mine], sy.at[mine], sysend, syrecv, dev(x, y2, z, c2)).start()

    def norms_wait():
        wait_bytes(sy.at[pl.ds(0, 7)], syrecv)

    def acts(side):
        if side == 1:
            rcopy(at.at[y], at.at[y], asend.at[0], a_dn, y_up).start()
        else:
            for h in range(2):
                rcopy(at.at[y, h], at.at[y, h], asend.at[1], a_up.at[h], y_dn).start()

    def act_relay(h):
        part = at.at[ys(1), h]
        wait_bytes(part, a_up.at[h])
        rcopy(part, part, afsend, a_far, y_dn).start()

    def scale():
        wait_bytes(at.at[ys(3)], a_dn)
        wait_bytes(at.at[ys(2)], a_far)
        for h in range(2):
            norm_ref[h] = jnp.max(jnp.sqrt(sy[y * 2 + h] + 1e-6))
        for h in range(2):
            for k in range(Y):
                factor = jnp.max(jnp.minimum(1.0, BOUND / jnp.sqrt(sy[ys(k) * 2 + h] + 1e-6)))
                scaled = (at[ys(k), h].astype(F32) * factor).astype(BF16)
                ats[:, pl.ds((h * Y + k) * SLOT_LEN, SLOT_LEN)] = scaled

    def chunk(xb, j):
        return gbuf.at[xb, :, c, j] if j < 2 else gbuf.at[xb, j - 2, c, pl.ds(2, 2)]

    def to_partner(xb, j):
        part = gbuf.at[xb, :, c, pl.ds(0, 2)] if j == 1 else chunk(xb, j)
        return rcopy(part, part, psend, precv.at[xb, j - 1], partner)

    def own_chunk(j):
        part = chunk(xb0, j)
        if j < 2:
            for q in range(NQ):
                wait_bytes(gbuf.at[xb0, q, c, j], yrecv.at[q, j])
        else:
            for k in (2, 3):
                wait_bytes(gbuf.at[xb0, j - 2, c, k], yrecv.at[j - 2, k])
        rcopy(part, part, kup.at[j], zrecv.at[xb0, j], z_up).start()
        rcopy(part, part, kdn.at[j], zrecv.at[xb0, j], z_dn).start()
        if j > 0:
            to_partner(xb0, j).start()

    def own_left(j):
        wait_bytes(chunk(xb0, j), kup.at[j])
        wait_bytes(chunk(xb0, j), kdn.at[j])

    def receive(side, d, j):
        xb = lax.div(zs(-d if side == 0 else d), 2)
        part = chunk(xb, j)
        wait_bytes(part, zrecv.at[xb, j])
        if d < 3 or (d == 3 and j % 2 == side):
            rcopy(part, part, zsend, zrecv.at[xb, j], (z_up, z_dn)[side]).start()
        if j > 0:
            to_partner(xb, j).start()

    def info(t):
        q_s = jnp.where(t < 2, t, jnp.where(t < 6, lax.div(t - 2, 2), t - 6))
        d_s = jnp.where(t < 2, 0, jnp.where(t < 6, 2, 4))
        q = jnp.where(is_src, q_s, lax.rem(lax.div(t, 2), 2))
        d = jnp.where(is_src, d_s, jnp.where(t < 4, 1, 3))
        z_from = lax.rem(jnp.where(lax.rem(t, 2) == 0, z + Z - d, z + d), Z)
        return lax.div(z_from, 2), q

    def relay_up(q):
        return rcopy(s2.at[q, pl.ds(0, 256)], rl.at[q], rsend.at[0], rlrecv.at[q], x_up)

    def relay_dn(q):
        return rcopy(s2.at[q, pl.ds(256, 256)], rr.at[q], rsend.at[1], rrrecv.at[q], x_dn)

    def final_up(q):
        return rcopy(s1.at[q], fl.at[q], fsend.at[0], flrecv.at[q], x_up)

    def final_dn(q):
        return rcopy(s3.at[q], fr.at[q], fsend.at[1], frrecv.at[q], x_dn)

    def consume(t):
        xb, q = info(t)

        @pl.when(q == 0)
        def _():
            wait_bytes(gbuf.at[xb, :, 1 - c, pl.ds(0, 2)], precv.at[xb, 0])

        wait_bytes(gbuf.at[xb, q, 1 - c, pl.ds(2, 2)], precv.at[xb, 1 + q])
        both = gbuf[xb, q].reshape(2 * Y * SLOT_LEN, W)
        part = jnp.dot(ats[...], both, preferred_element_type=F32) * (1.0 / SEQS)
        o = lax.rem(xb + X - x, X)

        @pl.when(o == 0)
        def _():
            own[q] = part

        @pl.when(o == 2)
        def _():
            s2[q] = part.astype(BF16)
            relay_up(q).start()
            relay_dn(q).start()

        @pl.when(lax.rem(o, 2) == 1)
        def _():
            hold[lax.rem(t, 2)] = part

    def finish(t):
        xb, q = info(t)
        o = lax.rem(xb + X - x, X)
        s = lax.rem(t, 2)

        @pl.when(o == 1)
        def _():
            relay_up(q).wait_recv()
            s1[q, pl.ds(0, 256)] = (hold[s, pl.ds(0, 256)] + rl[q].astype(F32)).astype(BF16)
            s1[q, pl.ds(256, 256)] = hold[s, pl.ds(256, 256)].astype(BF16)
            final_up(q).start()

        @pl.when(o == 3)
        def _():
            relay_dn(q).wait_recv()
            s3[q, pl.ds(0, 256)] = hold[s, pl.ds(0, 256)].astype(BF16)
            s3[q, pl.ds(256, 256)] = (hold[s, pl.ds(256, 256)] + rr[q].astype(F32)).astype(BF16)
            final_dn(q).start()

    calls = {
        "yl": first_steps, "yf": first_far, "o": own_chunk, "ol": own_left,
        "pairs": pair.start, "pairw": pair_wait, "ring": ring, "ringend": ring_end, "szs": squares,
        "szw": squares_wait, "syw": norms_wait, "aw": scale, "acts": acts, "arel": act_relay,
    }

    def run(plan):
        for name, *args in plan:
            if name == "r":
                receive(*args)
            else:
                calls[name](*args)

    rounds = {True: [[]], False: [[]]}
    for src, plan in ((True, SOURCE), (False, OTHER)):
        for item in plan:
            if item == ("C",):
                rounds[src].append([])
            else:
                rounds[src][-1].append(item)

    run(FIRST)

    @pl.when(is_src)
    def _():
        run(rounds[True][0])

    @pl.when(jnp.logical_not(is_src))
    def _():
        run(rounds[False][0])

    def round_of(t, _):
        for src in (True, False):
            for r in range(1, 8):
                if rounds[src][r]:
                    @pl.when(jnp.logical_and(t == r, is_src == src))
                    def _():
                        run(rounds[src][r])

        consume(t)

        @pl.when(t > 0)
        def _():
            finish(t - 1)

        return 0

    lax.fori_loop(0, 8, round_of, 0)
    finish(7)

    @pl.when(is_src)
    def _():
        for j in range(4):
            if ("ol", j) not in SOURCE:
                own_left(j)
        wait_bytes(gbuf.at[pl.ds(0, 2), :, c], zsend)

    @pl.when(jnp.logical_not(is_src))
    def _():
        wait_bytes(gbuf.at[pl.ds(0, 3), :, c], zsend)

    wait_bytes(gbuf.at[:, :, c], psend)

    @pl.when(steps_y == 0)
    def _():
        for q in range(NQ):
            first(q, 1 - c).wait_send()

    @pl.when(steps_y >= 1)
    def _():
        for q in range(NQ):
            first(q, 0).wait_send()
            first(q, 1).wait_send()

    pair.wait_send()
    for i in range(1, 5):
        ring_up(i).wait_send()
    for i in range(1, 4):
        ring_dn(i).wait_send()
    wait_bytes(sz.at[pl.ds(0, 7)], szsend)
    wait_bytes(sy.at[pl.ds(0, 7)], sysend)
    wait_bytes(at.at[y], asend.at[0])
    wait_bytes(at.at[y], asend.at[1])
    wait_bytes(at.at[y], afsend)
    wait_bytes(rl, rsend.at[0])
    wait_bytes(rr, rsend.at[1])

    for q in range(NQ):
        final_up(q).wait_recv()
        final_dn(q).wait_recv()
        block = own[q] + fl[q].astype(F32) + fr[q].astype(F32)
        out_ref[pl.ds(q * W, W), :] = block.T.astype(BF16)
    wait_bytes(s1, fsend.at[0])
    wait_bytes(s3, fsend.at[1])


def local(activations, out_grads, lengths):
    dma, vmem = pltpu.SemaphoreType.DMA, pltpu.VMEM
    grams = (2, 3, 16, 128)
    scratch = [
        vmem((2, SLOT_LEN, F), BF16),
        vmem((2, SLOT_LEN, F), BF16),
        vmem((X, NQ, 2, Y, SLOT_LEN, W), BF16),
        vmem((Y, 2, F, SLOT_LEN), BF16),
        vmem((F, 2 * Y * SLOT_LEN), BF16),
        vmem((2, Z) + grams, F32),
        vmem((Z,) + grams, F32),
        vmem((Z,) + grams, F32),
        vmem((4,) + grams, F32),
        vmem((3,) + grams, F32),
        vmem((3,) + grams, F32),
        vmem((2,) + grams, F32),
        vmem((Z, 8, 128), F32),
        vmem((2 * Y, 8, 128), F32),
        vmem((2, F, W), F32),
        vmem((NQ, F, W), F32),
        vmem((NQ, F, W), BF16),
        vmem((NQ, F, W), BF16),
        vmem((NQ, F, W), BF16),
        vmem((NQ, 256, W), BF16),
        vmem((NQ, 256, W), BF16),
        vmem((NQ, F, W), BF16),
        vmem((NQ, F, W), BF16),
        dma((2,)), dma((NQ, 2)), dma((NQ, Y)), dma((4,)), dma((4,)), dma, dma((X, 4)),
        dma, dma((X, 3)), dma((2,)), dma((2,)), dma, dma, dma,
        dma, dma, dma((4,)), dma((4,)), dma((3,)), dma((3,)), dma, dma, dma, dma,
        dma((2,)), dma((NQ,)), dma((NQ,)), dma((2,)), dma((NQ,)), dma((NQ,)),
    ]
    return pl.pallas_call(
        kernel,
        out_shape=(
            jax.ShapeDtypeStruct((F, F), BF16),
            jax.ShapeDtypeStruct((2,), F32),
        ),
        in_specs=[
            pl.BlockSpec(memory_space=pltpu.SMEM),
            pl.BlockSpec(memory_space=pl.ANY),
            pl.BlockSpec(memory_space=pl.ANY),
        ],
        out_specs=(
            pl.BlockSpec(memory_space=pltpu.VMEM),
            pl.BlockSpec(memory_space=pltpu.SMEM),
        ),
        scratch_shapes=scratch,
        compiler_params=pltpu.CompilerParams(
            collective_id=0, has_side_effects=True, vmem_limit_bytes=63 * 1024 * 1024 + 768 * 1024
        ),
        cost_estimate=pl.CostEstimate(flops=2 * 512 * 512 * 8192, bytes_accessed=3 * 2**19, transcendentals=0),
    )(lengths, activations, out_grads)


def solution(mesh):
    placed = (P("dp", None, "tensor"), P("dp", None, "tensor"), P("dp"))
    return jax.shard_map(
        local, mesh=mesh, in_specs=placed, out_specs=(P("dp", "tensor"), P("dp")), check_vma=False
    )
```

profile of v0, /device:TPU:4, one launch (start us, length us, event | category | flops | bytes accessed | tf_op | source)
XLA Modules:
  0.0 99.9 jit_solution(17455844375414075931)
XLA Ops:
  0.6 96.8 %shard_map.50 = (bf16[512,512]{1,0:T(8,128)(2,1)}, f32[2]{0:T(128)}) custom-call(s32[2]{0:T(128)} %len_ref.1, bf16[2,256,512]{2,1,0:T(8,128)(2,1)} %a_hbm.1, bf16[2,256,512]{2,1,0:T(8,128)(2,1)} %g_hbm.1), custom_call_target="tpu_custom_call" | custom-call | flops 4294967296 | bytes 1572864 | tf_op jit(solution)/shard_map/pallas_call | solution.py:443
  97.5 0.0 copy-start
  97.5 1.9 %copy.7 = bf16[512,512]{1,0:T(8,128)(2,1)} copy(bf16[512,512]{1,0:T(8,128)(2,1)} %get-tuple-element.4) | data formatting | bytes 1048576
  99.3 0.0 copy-done
  99.3 0.5 copy.8
Async XLA Ops:
  97.5 1.9 %copy-start = (f32[2]{0:T(128)S(1)}, f32[2]{0:T(128)}, u32[]{:S(2)}) copy-start(f32[2]{0:T(128)} %get-tuple-element.5) | copy-start | bytes 28
where the time goes:
time: 100 us; the launch traced here: 99.9 us
  Pallas kernels  96.8 us (97%)
  local copies, waits for them, and re-layouts  2.38 us (2%)
    pallas_call x1, Pallas kernels, local(): pl.pallas_call(kernel, out_shape=(jax.ShapeDtypeStruct((F, F), BF16), jax...  96.8 us
    unnamed x4, local copies, waits for them, and re-layouts  2.38 us

commit v1 on v0

--- a/solution.py
+++ b/solution.py
@@ -291,12 +291,12 @@
 
         @pl.when(lax.rem(o, 2) == 1)
         def _():
-            hold[lax.rem(t, 2)] = part
+            hold[lax.rem(t, 3)] = part
 
     def finish(t):
         xb, q = info(t)
         o = lax.rem(xb + X - x, X)
-        s = lax.rem(t, 2)
+        s = lax.rem(t, 3)
 
         @pl.when(o == 1)
         def _():
@@ -353,13 +353,14 @@
 
         consume(t)
 
-        @pl.when(t > 0)
-        def _():
-            finish(t - 1)
+        @pl.when(t > 1)
+        def _():
+            finish(t - 2)
 
         return 0
 
     lax.fori_loop(0, 8, round_of, 0)
+    finish(6)
     finish(7)
 
     @pl.when(is_src)
@@ -426,7 +427,7 @@
         vmem((2,) + grams, F32),
         vmem((Z, 8, 128), F32),
         vmem((2 * Y, 8, 128), F32),
-        vmem((2, F, W), F32),
+        vmem((3, F, W), F32),
         vmem((NQ, F, W), F32),
         vmem((NQ, F, W), BF16),
         vmem((NQ, F, W), BF16),
@@ -457,10 +458,10 @@
         ),
         scratch_shapes=scratch,
         compiler_params=pltpu.CompilerParams(
-            collective_id=0, has_side_effects=True, vmem_limit_bytes=63 * 1024 * 1024 + 768 * 1024
+            collective_id=0, has_side_effects=True, vmem_limit_bytes=40 * 1024 * 1024
         ),
         cost_estimate=pl.CostEstimate(flops=2 * 512 * 512 * 8192, bytes_accessed=3 * 2**19, transcendentals=0),
-    )(lengths, activations, out_grads)
+    )(*(pltpu.with_memory_space_constraint(v, pltpu.HBM) for v in (lengths, activations, out_grads)))
 
 
 def solution(mesh):

time: 100 us -> 92.1 us (0.921)
  Pallas kernels: 96.8 us -> 90 us
  local copies, waits for them, and re-layouts: 2.38 us -> 1.31 us
    pallas_call x1, Pallas kernels: 96.8 us -> 90 us  [local(): pl.pallas_call(kernel, out_shape=(jax.ShapeDtypeStruct((F, F), BF16), jax...]
    unnamed x4 -> x2, local copies, waits for them, and re-layouts: 2.38 us -> 1.31 us
where the time goes in v1:
time: 92.1 us; the launch traced here: 91.9 us
  Pallas kernels  90 us (98%)
  local copies, waits for them, and re-layouts  1.31 us (1%)
    pallas_call x1, Pallas kernels, local(): pl.pallas_call(kernel, out_shape=(jax.ShapeDtypeStruct((F, F), BF16), jax...  90 us

profile of v1, /device:TPU:4, one launch (start us, length us, event | category | flops | bytes accessed | tf_op | source)
XLA Modules:
  0.0 91.9 jit_solution(10100463372554247706)
XLA Ops:
  0.6 90.0 %shard_map.50 = (bf16[512,512]{1,0:T(8,128)(2,1)S(1)}, f32[2]{0:T(128)S(1)}) custom-call(s32[2]{0:T(128)} %len_ref.1, bf16[2,256,512]{2,1,0:T(8,128)(2,1)} %a_hbm.1, bf16[2,256,512]{2,1,0:T(8,128)(2,1)} %g_hbm.1), custom_call_target="tpu_custom_call" | custom-call | flops 4294967296 | bytes 1572864 | tf_op jit(solution)/shard_map/pallas_call | solution.py:444
  90.6 0.8 copy.7
  91.4 0.5 copy.8

commit v2 on v1

--- a/solution.py
+++ b/solution.py
@@ -20,21 +20,21 @@
 BF16 = jnp.bfloat16
 
 FIRST = (
-    ("pairs",), ("yl",), ("yf", 0),
+    ("yl",), ("gram",), ("yf", 0), ("pairs",),
 )
 SOURCE = (
-    ("o", 0), ("pairw",), ("ring", 1), ("yf", 1), ("ring", 2), ("o", 1), ("ring", 3), ("acts", 3),
-    ("acts", 1), ("ring", 4), ("o", 2), ("ringend",), ("szs",), ("o", 3), ("r", 1, 2, 0), ("r", 0, 2, 0),
-    ("arel", 0), ("arel", 1), ("szw",), ("r", 0, 2, 1), ("r", 1, 2, 1), ("syw",), ("aw",), ("r", 1, 2, 2),
-    ("C",), ("r", 0, 2, 2), ("C",), ("r", 1, 2, 3), ("C",), ("r", 0, 2, 3), ("C",), ("C",), ("C",),
+    ("o", 0), ("yf", 1), ("pairw",), ("ring", 1), ("ring", 2), ("o", 1), ("acts", 3), ("ring", 3),
+    ("ring", 4), ("o", 2), ("acts", 1), ("ringend",), ("szs",), ("o", 3), ("r", 1, 2, 0), ("r", 0, 2, 0),
+    ("arel", 0), ("arel", 1), ("szw",), ("r", 1, 2, 1), ("r", 0, 2, 1), ("syw",), ("aw",), ("C",),
+    ("r", 1, 2, 2), ("r", 0, 2, 2), ("C",), ("C",), ("r", 1, 2, 3), ("C",), ("r", 0, 2, 3), ("C",), ("C",),
     ("r", 0, 4, 0), ("r", 1, 4, 1), ("r", 0, 4, 2), ("C",), ("r", 1, 4, 3), ("C",),
 )
 OTHER = (
-    ("pairw",), ("ring", 1), ("yf", 1), ("ring", 2), ("ring", 3), ("acts", 3), ("r", 0, 1, 0), ("r", 1, 1, 0),
-    ("acts", 1), ("ring", 4), ("ringend",), ("szs",), ("r", 1, 1, 1), ("r", 0, 1, 1), ("arel", 0),
-    ("arel", 1), ("szw",), ("r", 1, 1, 2), ("r", 0, 1, 2), ("r", 1, 1, 3), ("r", 0, 1, 3), ("syw",), ("aw",),
-    ("C",), ("r", 1, 3, 0), ("C",), ("r", 0, 3, 0), ("C",), ("C",), ("r", 1, 3, 1), ("r", 0, 3, 1),
-    ("r", 1, 3, 2), ("r", 0, 3, 2), ("C",), ("r", 1, 3, 3), ("r", 0, 3, 3), ("C",), ("C",), ("C",),
+    ("pairw",), ("yf", 1), ("ring", 1), ("ring", 2), ("acts", 3), ("ring", 3), ("r", 0, 1, 0), ("r", 1, 1, 0),
+    ("ring", 4), ("acts", 1), ("ringend",), ("szs",), ("r", 1, 1, 1), ("r", 0, 1, 1), ("arel", 0),
+    ("arel", 1), ("szw",), ("r", 0, 1, 2), ("r", 1, 1, 2), ("r", 1, 1, 3), ("syw",), ("r", 0, 1, 3), ("aw",),
+    ("C",), ("C",), ("r", 1, 3, 0), ("r", 0, 3, 0), ("C",), ("C",), ("r", 1, 3, 1), ("r", 0, 3, 1),
+    ("r", 0, 3, 2), ("r", 1, 3, 2), ("C",), ("r", 1, 3, 3), ("C",), ("r", 0, 3, 3), ("C",), ("C",),
 )
 
 def rcopy(src, dst, send, recv, device):
@@ -97,7 +97,8 @@
     contract = (((1,), (1,)), ((), ()))
     load_a.wait()
     load_g.wait()
-    for s in range(2):
+
+    def gram(s):
         am = jnp.where(rows < len_ref[s], a_ref[s].astype(F32), 0.0)
         at[y, s] = am.T.astype(BF16)
         am = am.astype(BF16)
@@ -107,6 +108,7 @@
             gpack[s, :, m, 0] = full[:128, :128].reshape(Z, 16, 128)
             gpack[s, :, m, 1] = full[:128, 128:].reshape(Z, 16, 128)
             gpack[s, :, m, 2] = full[128:, 128:].reshape(Z, 16, 128)
+    gram(0)
     pl.semaphore_wait(barrier, len(peers))
 
     xb0 = lax.div(z, 2)
@@ -255,17 +257,33 @@
         z_from = lax.rem(jnp.where(lax.rem(t, 2) == 0, z + Z - d, z + d), Z)
         return lax.div(z_from, 2), q
 
-    def relay_up(q):
-        return rcopy(s2.at[q, pl.ds(0, 256)], rl.at[q], rsend.at[0], rlrecv.at[q], x_up)
-
-    def relay_dn(q):
-        return rcopy(s2.at[q, pl.ds(256, 256)], rr.at[q], rsend.at[1], rrrecv.at[q], x_dn)
-
-    def final_up(q):
-        return rcopy(s1.at[q], fl.at[q], fsend.at[0], flrecv.at[q], x_up)
-
-    def final_dn(q):
-        return rcopy(s3.at[q], fr.at[q], fsend.at[1], frrecv.at[q], x_dn)
+    def relay_up(q, first, rows, slot):
+        part = pl.ds(first, rows)
+        return rcopy(s2.at[q, part], rl.at[q, part], rsend.at[0], rlrecv.at[q, slot], x_up)
+
+    def relay_dn(q, first, rows, slot):
+        return rcopy(
+            s2.at[q, pl.ds(256 + first, rows)], rr.at[q, pl.ds(first, rows)], rsend.at[1],
+            rrrecv.at[q, slot], x_dn,
+        )
+
+    def final_up(q, first, rows):
+        part = pl.ds(first, rows)
+        rcopy(s1.at[q, part], fl.at[q, part], fsend.at[0], flrecv.at[q], x_up).start()
+
+    def final_dn(q, first, rows):
+        part = pl.ds(first, rows)
+        rcopy(s3.at[q, part], fr.at[q, part], fsend.at[1], frrecv.at[q], x_dn).start()
+
+    def parts_of(t, run_part):
+        @pl.when(t < 6)
+        def _():
+            run_part(0, 256, 0)
+
+        @pl.when(t >= 6)
+        def _():
+            run_part(0, 128, 0)
+            run_part(128, 128, 1)
 
     def consume(t):
         xb, q = info(t)
@@ -286,12 +304,24 @@
         @pl.when(o == 2)
         def _():
             s2[q] = part.astype(BF16)
-            relay_up(q).start()
-            relay_dn(q).start()
-
-        @pl.when(lax.rem(o, 2) == 1)
-        def _():
-            hold[lax.rem(t, 3)] = part
+
+            def send(first, rows, slot):
+                relay_up(q, first, rows, slot).start()
+                relay_dn(q, first, rows, slot).start()
+
+            parts_of(t, send)
+
+        @pl.when(o == 1)
+        def _():
+            s1[q, pl.ds(256, 256)] = part[256:].astype(BF16)
+            final_up(q, 256, 256)
+            hold[lax.rem(t, 3)] = part[:256]
+
+        @pl.when(o == 3)
+        def _():
+            s3[q, pl.ds(0, 256)] = part[:256].astype(BF16)
+            final_dn(q, 0, 256)
+            hold[lax.rem(t, 3)] = part[256:]
 
     def finish(t):
         xb, q = info(t)
@@ -300,20 +330,26 @@
 
         @pl.when(o == 1)
         def _():
-            relay_up(q).wait_recv()
-            s1[q, pl.ds(0, 256)] = (hold[s, pl.ds(0, 256)] + rl[q].astype(F32)).astype(BF16)
-            s1[q, pl.ds(256, 256)] = hold[s, pl.ds(256, 256)].astype(BF16)
-            final_up(q).start()
+            def add(first, rows, slot):
+                part = pl.ds(first, rows)
+                relay_up(q, first, rows, slot).wait_recv()
+                s1[q, part] = (hold[s, part] + rl[q, part].astype(F32)).astype(BF16)
+                final_up(q, first, rows)
+
+            parts_of(t, add)
 
         @pl.when(o == 3)
         def _():
-            relay_dn(q).wait_recv()
-            s3[q, pl.ds(0, 256)] = hold[s, pl.ds(0, 256)].astype(BF16)
-            s3[q, pl.ds(256, 256)] = (hold[s, pl.ds(256, 256)] + rr[q].astype(F32)).astype(BF16)
-            final_dn(q).start()
+            def add(first, rows, slot):
+                part = pl.ds(first, rows)
+                relay_dn(q, first, rows, slot).wait_recv()
+                s3[q, pl.ds(256 + first, rows)] = (hold[s, part] + rr[q, part].astype(F32)).astype(BF16)
+                final_dn(q, 256 + first, rows)
+
+            parts_of(t, add)
 
     calls = {
-        "yl": first_steps, "yf": first_far, "o": own_chunk, "ol": own_left,
+        "gram": lambda: gram(1), "yl": first_steps, "yf": first_far, "o": own_chunk, "ol": own_left,
         "pairs": pair.start, "pairw": pair_wait, "ring": ring, "ringend": ring_end, "szs": squares,
         "szw": squares_wait, "syw": norms_wait, "aw": scale, "acts": acts, "arel": act_relay,
     }
@@ -401,8 +437,8 @@
     wait_bytes(rr, rsend.at[1])
 
     for q in range(NQ):
-        final_up(q).wait_recv()
-        final_dn(q).wait_recv()
+        wait_bytes(fl.at[q], flrecv.at[q])
+        wait_bytes(fr.at[q], frrecv.at[q])
         block = own[q] + fl[q].astype(F32) + fr[q].astype(F32)
         out_ref[pl.ds(q * W, W), :] = block.T.astype(BF16)
     wait_bytes(s1, fsend.at[0])
@@ -427,7 +463,7 @@
         vmem((2,) + grams, F32),
         vmem((Z, 8, 128), F32),
         vmem((2 * Y, 8, 128), F32),
-        vmem((3, F, W), F32),
+        vmem((3, 256, W), F32),
         vmem((NQ, F, W), F32),
         vmem((NQ, F, W), BF16),
         vmem((NQ, F, W), BF16),
@@ -439,7 +475,7 @@
         dma((2,)), dma((NQ, 2)), dma((NQ, Y)), dma((4,)), dma((4,)), dma, dma((X, 4)),
         dma, dma((X, 3)), dma((2,)), dma((2,)), dma, dma, dma,
         dma, dma, dma((4,)), dma((4,)), dma((3,)), dma((3,)), dma, dma, dma, dma,
-        dma((2,)), dma((NQ,)), dma((NQ,)), dma((2,)), dma((NQ,)), dma((NQ,)),
+        dma((2,)), dma((NQ, 2)), dma((NQ, 2)), dma((2,)), dma((NQ,)), dma((NQ,)),
     ]
     return pl.pallas_call(
         kernel,

time: 92.1 us -> 87.1 us (0.946)
  the two profiles are of different devices: /device:TPU:4 before, /device:TPU:12 now
where the time goes in v2:
time: 87.1 us; the launch traced here: 87 us
  Pallas kernels  85 us (98%)
  local copies, waits for them, and re-layouts  1.31 us (2%)
    pallas_call x1, Pallas kernels, local(): pl.pallas_call(kernel, out_shape=(jax.ShapeDtypeStruct((F, F), BF16), jax...  85 us

profile of v2, /device:TPU:12, one launch (start us, length us, event | category | flops | bytes accessed | tf_op | source)
XLA Modules:
  0.0 87.0 jit_solution(4044359693564572811)
XLA Ops:
  0.6 85.0 %shard_map.50 = (bf16[512,512]{1,0:T(8,128)(2,1)S(1)}, f32[2]{0:T(128)S(1)}) custom-call(s32[2]{0:T(128)} %len_ref.1, bf16[2,256,512]{2,1,0:T(8,128)(2,1)} %a_hbm.1, bf16[2,256,512]{2,1,0:T(8,128)(2,1)} %g_hbm.1), custom_call_target="tpu_custom_call" | custom-call | flops 4294967296 | bytes 1572864 | tf_op jit(solution)/shard_map/pallas_call | solution.py:480
  85.6 0.8 copy.7
  86.4 0.5 copy.8

commit v3 on v2

--- a/solution.py
+++ b/solution.py
@@ -20,21 +20,23 @@
 BF16 = jnp.bfloat16
 
 FIRST = (
-    ("yl",), ("gram",), ("yf", 0), ("pairs",),
+    ("yl",),
 )
 SOURCE = (
-    ("o", 0), ("yf", 1), ("pairw",), ("ring", 1), ("ring", 2), ("o", 1), ("acts", 3), ("ring", 3),
-    ("ring", 4), ("o", 2), ("acts", 1), ("ringend",), ("szs",), ("o", 3), ("r", 1, 2, 0), ("r", 0, 2, 0),
-    ("arel", 0), ("arel", 1), ("szw",), ("r", 1, 2, 1), ("r", 0, 2, 1), ("syw",), ("aw",), ("C",),
-    ("r", 1, 2, 2), ("r", 0, 2, 2), ("C",), ("C",), ("r", 1, 2, 3), ("C",), ("r", 0, 2, 3), ("C",), ("C",),
-    ("r", 0, 4, 0), ("r", 1, 4, 1), ("r", 0, 4, 2), ("C",), ("r", 1, 4, 3), ("C",),
+    ("gram",), ("o", 0), ("pairs",), ("yf", 0), ("pairw",), ("ring", 1), ("yg", 0), ("ring", 2), ("yg", 1),
+    ("yf", 1), ("acts", 3), ("o", 1), ("ring", 3), ("ring", 4), ("o", 2), ("ringend",), ("szs",), ("acts", 1),
+    ("o", 3), ("r", 0, 2, 0), ("r", 1, 2, 0), ("arel", 0), ("szw",), ("arel", 1), ("r", 1, 2, 1),
+    ("r", 0, 2, 1), ("syw",), ("r", 1, 2, 2), ("aw",), ("C",), ("r", 0, 2, 2), ("C",), ("C",), ("C",),
+    ("r", 1, 2, 3), ("r", 0, 2, 3), ("C",), ("r", 0, 4, 0), ("C",), ("r", 1, 4, 1), ("r", 0, 4, 2), ("C",),
+    ("r", 1, 4, 3), ("C",),
 )
 OTHER = (
-    ("pairw",), ("yf", 1), ("ring", 1), ("ring", 2), ("acts", 3), ("ring", 3), ("r", 0, 1, 0), ("r", 1, 1, 0),
-    ("ring", 4), ("acts", 1), ("ringend",), ("szs",), ("r", 1, 1, 1), ("r", 0, 1, 1), ("arel", 0),
-    ("arel", 1), ("szw",), ("r", 0, 1, 2), ("r", 1, 1, 2), ("r", 1, 1, 3), ("syw",), ("r", 0, 1, 3), ("aw",),
-    ("C",), ("C",), ("r", 1, 3, 0), ("r", 0, 3, 0), ("C",), ("C",), ("r", 1, 3, 1), ("r", 0, 3, 1),
-    ("r", 0, 3, 2), ("r", 1, 3, 2), ("C",), ("r", 1, 3, 3), ("C",), ("r", 0, 3, 3), ("C",), ("C",),
+    ("yf", 0), ("gram",), ("pairs",), ("pairw",), ("ring", 1), ("yg", 0), ("yg", 1), ("yf", 1), ("ring", 2),
+    ("acts", 3), ("ring", 3), ("r", 1, 1, 0), ("r", 0, 1, 0), ("ring", 4), ("ringend",), ("szs",),
+    ("acts", 1), ("r", 1, 1, 1), ("r", 0, 1, 1), ("arel", 0), ("szw",), ("arel", 1), ("r", 1, 1, 2),
+    ("r", 0, 1, 2), ("syw",), ("r", 0, 1, 3), ("r", 1, 1, 3), ("aw",), ("r", 1, 3, 0), ("C",), ("r", 0, 3, 0),
+    ("C",), ("C",), ("C",), ("r", 0, 3, 1), ("r", 1, 3, 1), ("r", 0, 3, 2), ("r", 1, 3, 2), ("C",), ("C",),
+    ("r", 1, 3, 3), ("r", 0, 3, 3), ("C",), ("C",),
 )
 
 def rcopy(src, dst, send, recv, device):
@@ -137,8 +139,8 @@
                 first(q, 0).start()
                 first(q, 1).start()
 
-    def first_far(q):
-        @pl.when(steps_y >= 2)
+    def first_far(steps, q):
+        @pl.when(steps_y == steps)
         def _():
             first(q, 0).start()
             first(q, 1).start()
@@ -195,18 +197,18 @@
 
     def acts(side):
         if side == 1:
-            rcopy(at.at[y], at.at[y], asend.at[0], a_dn, y_up).start()
+            rcopy(at.at[y], at.at[y], asend.at[0], a_dn, y_dn).start()
         else:
             for h in range(2):
-                rcopy(at.at[y, h], at.at[y, h], asend.at[1], a_up.at[h], y_dn).start()
+                rcopy(at.at[y, h], at.at[y, h], asend.at[1], a_up.at[h], y_up).start()
 
     def act_relay(h):
-        part = at.at[ys(1), h]
+        part = at.at[ys(3), h]
         wait_bytes(part, a_up.at[h])
-        rcopy(part, part, afsend, a_far, y_dn).start()
+        rcopy(part, part, afsend, a_far, y_up).start()
 
     def scale():
-        wait_bytes(at.at[ys(3)], a_dn)
+        wait_bytes(at.at[ys(1)], a_dn)
         wait_bytes(at.at[ys(2)], a_far)
         for h in range(2):
             norm_ref[h] = jnp.max(jnp.sqrt(sy[y * 2 + h] + 1e-6))
@@ -349,7 +351,7 @@
             parts_of(t, add)
 
     calls = {
-        "gram": lambda: gram(1), "yl": first_steps, "yf": first_far, "o": own_chunk, "ol": own_left,
+        "gram": lambda: gram(1), "yl": first_steps, "yf": lambda q: first_far(3, q), "yg": lambda q: first_far(2, q), "o": own_chunk, "ol": own_left,
         "pairs": pair.start, "pairw": pair_wait, "ring": ring, "ringend": ring_end, "szs": squares,
         "szw": squares_wait, "syw": norms_wait, "aw": scale, "acts": acts, "arel": act_relay,
     }

time: 87.1 us -> 88.8 us (1.020)
  the two profiles are of different devices: /device:TPU:12 before, /device:TPU:4 now
where the time goes in v3:
time: 88.8 us; the launch traced here: 88.4 us
  Pallas kernels  86.5 us (97%)
  local copies, waits for them, and re-layouts  1.31 us (1%)
    pallas_call x1, Pallas kernels, local(): pl.pallas_call(kernel, out_shape=(jax.ShapeDtypeStruct((F, F), BF16), jax...  86.5 us

profile of v3, /device:TPU:4, one launch (start us, length us, event | category | flops | bytes accessed | tf_op | source)
XLA Modules:
  0.0 88.4 jit_solution(4041552092927026785)
XLA Ops:
  0.6 86.5 %shard_map.50 = (bf16[512,512]{1,0:T(8,128)(2,1)S(1)}, f32[2]{0:T(128)S(1)}) custom-call(s32[2]{0:T(128)} %len_ref.1, bf16[2,256,512]{2,1,0:T(8,128)(2,1)} %a_hbm.1, bf16[2,256,512]{2,1,0:T(8,128)(2,1)} %g_hbm.1), custom_call_target="tpu_custom_call" | custom-call | flops 4294967296 | bytes 1572864 | tf_op jit(solution)/shard_map/pallas_call | solution.py:482
  87.1 0.8 copy.7
  87.9 0.5 copy.8

commit v4 on v3

--- a/solution.py
+++ b/solution.py
@@ -23,20 +23,20 @@
     ("yl",),
 )
 SOURCE = (
-    ("gram",), ("o", 0), ("pairs",), ("yf", 0), ("pairw",), ("ring", 1), ("yg", 0), ("ring", 2), ("yg", 1),
-    ("yf", 1), ("acts", 3), ("o", 1), ("ring", 3), ("ring", 4), ("o", 2), ("ringend",), ("szs",), ("acts", 1),
-    ("o", 3), ("r", 0, 2, 0), ("r", 1, 2, 0), ("arel", 0), ("szw",), ("arel", 1), ("r", 1, 2, 1),
-    ("r", 0, 2, 1), ("syw",), ("r", 1, 2, 2), ("aw",), ("C",), ("r", 0, 2, 2), ("C",), ("C",), ("C",),
-    ("r", 1, 2, 3), ("r", 0, 2, 3), ("C",), ("r", 0, 4, 0), ("C",), ("r", 1, 4, 1), ("r", 0, 4, 2), ("C",),
-    ("r", 1, 4, 3), ("C",),
+    ("yf", 0), ("gram",), ("pairs",), ("o", 0), ("pairw",), ("yf", 1), ("ring", 1), ("yg", 0), ("ring", 2),
+    ("yg", 1), ("o", 1), ("acts", 3), ("ring", 3), ("acts", 1), ("o", 2), ("ring", 4), ("ringend",), ("szs",),
+    ("r", 1, 2, 0), ("o", 3), ("r", 0, 2, 0), ("arel", 0), ("arel", 1), ("szw",), ("r", 1, 2, 1), ("syw",),
+    ("r", 0, 2, 1), ("aw",), ("C",), ("r", 1, 2, 2), ("r", 0, 2, 2), ("C",), ("C",), ("C",), ("r", 1, 2, 3),
+    ("r", 0, 2, 3), ("r", 0, 4, 0), ("C",), ("C",), ("r", 1, 4, 1), ("r", 0, 4, 2), ("C",), ("r", 1, 4, 3),
+    ("C",),
 )
 OTHER = (
-    ("yf", 0), ("gram",), ("pairs",), ("pairw",), ("ring", 1), ("yg", 0), ("yg", 1), ("yf", 1), ("ring", 2),
-    ("acts", 3), ("ring", 3), ("r", 1, 1, 0), ("r", 0, 1, 0), ("ring", 4), ("ringend",), ("szs",),
-    ("acts", 1), ("r", 1, 1, 1), ("r", 0, 1, 1), ("arel", 0), ("szw",), ("arel", 1), ("r", 1, 1, 2),
-    ("r", 0, 1, 2), ("syw",), ("r", 0, 1, 3), ("r", 1, 1, 3), ("aw",), ("r", 1, 3, 0), ("C",), ("r", 0, 3, 0),
-    ("C",), ("C",), ("C",), ("r", 0, 3, 1), ("r", 1, 3, 1), ("r", 0, 3, 2), ("r", 1, 3, 2), ("C",), ("C",),
-    ("r", 1, 3, 3), ("r", 0, 3, 3), ("C",), ("C",),
+    ("yf", 0), ("gram",), ("pairs",), ("pairw",), ("ring", 1), ("yf", 1), ("yg", 0), ("ring", 2), ("acts", 3),
+    ("r", 0, 1, 0), ("yg", 1), ("ring", 3), ("r", 1, 1, 0), ("acts", 1), ("ring", 4), ("r", 1, 1, 1),
+    ("r", 0, 1, 1), ("arel", 0), ("ringend",), ("szs",), ("arel", 1), ("r", 1, 1, 2), ("r", 0, 1, 2),
+    ("szw",), ("syw",), ("aw",), ("r", 1, 3, 0), ("C",), ("r", 1, 1, 3), ("r", 0, 1, 3), ("C",),
+    ("r", 0, 3, 0), ("C",), ("C",), ("r", 1, 3, 1), ("r", 0, 3, 1), ("r", 1, 3, 2), ("r", 0, 3, 2), ("C",),
+    ("r", 1, 3, 3), ("C",), ("r", 0, 3, 3), ("C",), ("C",),
 )
 
 def rcopy(src, dst, send, recv, device):
@@ -58,7 +58,7 @@
     len_ref, a_hbm, g_hbm, out_ref, norm_ref,
     a_ref, g_ref, gbuf, at, ats, gpack, gpair, gsum, gup, gdn, sup, sdn, sz, sy,
     hold, own, s1, s2, s3, rl, rr, fl, fr,
-    loads, ysend, yrecv, kup, kdn, zsend, zrecv, psend, precv, asend, a_up, a_dn, a_far, afsend,
+    loads, ysend, yrecv, kup, kdn, zsend, zrecv, psend, precv, asend, a_near, a_other, a_far, afsend,
     gpsend, gprecv, gupsend, guprecv, gdnsend, gdnrecv, szsend, szrecv, sysend, syrecv,
     rsend, rlrecv, rrrecv, fsend, flrecv, frrecv,
 ):
@@ -195,21 +195,23 @@
     def norms_wait():
         wait_bytes(sy.at[pl.ds(0, 7)], syrecv)
 
-    def acts(side):
-        if side == 1:
-            rcopy(at.at[y], at.at[y], asend.at[0], a_dn, y_dn).start()
-        else:
-            for h in range(2):
-                rcopy(at.at[y, h], at.at[y, h], asend.at[1], a_up.at[h], y_up).start()
+    def act(h, way):
+        sem = a_near.at[h] if h == way else a_other.at[h]
+        rcopy(at.at[y, h], at.at[y, h], asend.at[way], sem, (y_up, y_dn)[way]).start()
+
+    def acts(which):
+        for way in range(2):
+            act(way if which == 3 else 1 - way, way)
 
     def act_relay(h):
-        part = at.at[ys(3), h]
-        wait_bytes(part, a_up.at[h])
-        rcopy(part, part, afsend, a_far, y_up).start()
+        part = at.at[ys(3 - 2 * h), h]
+        wait_bytes(part, a_near.at[h])
+        rcopy(part, part, afsend.at[h], a_far.at[h], (y_up, y_dn)[h]).start()
 
     def scale():
-        wait_bytes(at.at[ys(1)], a_dn)
-        wait_bytes(at.at[ys(2)], a_far)
+        for h in range(2):
+            wait_bytes(at.at[ys(1 + 2 * h), h], a_other.at[h])
+            wait_bytes(at.at[ys(2), h], a_far.at[h])
         for h in range(2):
             norm_ref[h] = jnp.max(jnp.sqrt(sy[y * 2 + h] + 1e-6))
         for h in range(2):
@@ -434,7 +436,8 @@
     wait_bytes(sy.at[pl.ds(0, 7)], sysend)
     wait_bytes(at.at[y], asend.at[0])
     wait_bytes(at.at[y], asend.at[1])
-    wait_bytes(at.at[y], afsend)
+    for h in range(2):
+        wait_bytes(at.at[y, h], afsend.at[h])
     wait_bytes(rl, rsend.at[0])
     wait_bytes(rr, rsend.at[1])
 
@@ -475,7 +478,7 @@
         vmem((NQ, F, W), BF16),
         vmem((NQ, F, W), BF16),
         dma((2,)), dma((NQ, 2)), dma((NQ, Y)), dma((4,)), dma((4,)), dma, dma((X, 4)),
-        dma, dma((X, 3)), dma((2,)), dma((2,)), dma, dma, dma,
+        dma, dma((X, 3)), dma((2,)), dma((2,)), dma((2,)), dma((2,)), dma((2,)),
         dma, dma, dma((4,)), dma((4,)), dma((3,)), dma((3,)), dma, dma, dma, dma,
         dma((2,)), dma((NQ, 2)), dma((NQ, 2)), dma((2,)), dma((NQ,)), dma((NQ,)),
     ]

time: 88.8 us -> 85 us (0.957)
  Pallas kernels: 86.5 us -> 82.2 us
    pallas_call x1, Pallas kernels: 86.5 us -> 82.2 us  [local(): pl.pallas_call(kernel, out_shape=(jax.ShapeDtypeStruct((F, F), BF16), jax...]
where the time goes in v4:
time: 85 us; the launch traced here: 84.1 us
  Pallas kernels  82.2 us (97%)
  local copies, waits for them, and re-layouts  1.31 us (2%)
    pallas_call x1, Pallas kernels, local(): pl.pallas_call(kernel, out_shape=(jax.ShapeDtypeStruct((F, F), BF16), jax...  82.2 us

profile of v4, /device:TPU:4, one launch (start us, length us, event | category | flops | bytes accessed | tf_op | source)
XLA Modules:
  0.0 84.1 jit_solution(15790732288064862413)
XLA Ops:
  0.6 82.2 %shard_map.50 = (bf16[512,512]{1,0:T(8,128)(2,1)S(1)}, f32[2]{0:T(128)S(1)}) custom-call(s32[2]{0:T(128)} %len_ref.1, bf16[2,256,512]{2,1,0:T(8,128)(2,1)} %a_hbm.1, bf16[2,256,512]{2,1,0:T(8,128)(2,1)} %g_hbm.1), custom_call_target="tpu_custom_call" | custom-call | flops 4294967296 | bytes 1572864 | tf_op jit(solution)/shard_map/pallas_call | solution.py:485
  82.8 0.8 copy.7
  83.6 0.5 copy.8

commit v5 on v4

--- a/solution.py
+++ b/solution.py
@@ -23,20 +23,20 @@
     ("yl",),
 )
 SOURCE = (
-    ("yf", 0), ("gram",), ("pairs",), ("o", 0), ("pairw",), ("yf", 1), ("ring", 1), ("yg", 0), ("ring", 2),
-    ("yg", 1), ("o", 1), ("acts", 3), ("ring", 3), ("acts", 1), ("o", 2), ("ring", 4), ("ringend",), ("szs",),
-    ("r", 1, 2, 0), ("o", 3), ("r", 0, 2, 0), ("arel", 0), ("arel", 1), ("szw",), ("r", 1, 2, 1), ("syw",),
-    ("r", 0, 2, 1), ("aw",), ("C",), ("r", 1, 2, 2), ("r", 0, 2, 2), ("C",), ("C",), ("C",), ("r", 1, 2, 3),
-    ("r", 0, 2, 3), ("r", 0, 4, 0), ("C",), ("C",), ("r", 1, 4, 1), ("r", 0, 4, 2), ("C",), ("r", 1, 4, 3),
-    ("C",),
+    ("gram",), ("pairs",), ("o", 0), ("yf", 0), ("pairw",), ("yf", 1), ("yg", 0), ("ring", 1), ("acts", 1),
+    ("acts", 3), ("ring", 2), ("o", 1), ("ring", 3), ("o", 2), ("ring", 4), ("yg", 1), ("ringend",), ("szs",),
+    ("r", 1, 2, 0), ("r", 0, 2, 0), ("o", 3), ("arel", 0), ("arel", 1), ("szw",), ("r", 1, 2, 1), ("syw",),
+    ("aw",), ("r", 0, 2, 1), ("C",), ("r", 1, 2, 2), ("r", 0, 2, 2), ("C",), ("C",), ("C",), ("r", 1, 2, 3),
+    ("r", 0, 2, 3), ("r", 0, 4, 0), ("C",), ("C",), ("r", 1, 4, 1), ("r", 0, 4, 2), ("E", 6), ("C",),
+    ("E", 7), ("r", 1, 4, 3), ("C",),
 )
 OTHER = (
-    ("yf", 0), ("gram",), ("pairs",), ("pairw",), ("ring", 1), ("yf", 1), ("yg", 0), ("ring", 2), ("acts", 3),
+    ("yf", 0), ("gram",), ("pairs",), ("pairw",), ("ring", 1), ("yg", 0), ("ring", 2), ("acts", 3), ("yf", 1),
     ("r", 0, 1, 0), ("yg", 1), ("ring", 3), ("r", 1, 1, 0), ("acts", 1), ("ring", 4), ("r", 1, 1, 1),
-    ("r", 0, 1, 1), ("arel", 0), ("ringend",), ("szs",), ("arel", 1), ("r", 1, 1, 2), ("r", 0, 1, 2),
-    ("szw",), ("syw",), ("aw",), ("r", 1, 3, 0), ("C",), ("r", 1, 1, 3), ("r", 0, 1, 3), ("C",),
-    ("r", 0, 3, 0), ("C",), ("C",), ("r", 1, 3, 1), ("r", 0, 3, 1), ("r", 1, 3, 2), ("r", 0, 3, 2), ("C",),
-    ("r", 1, 3, 3), ("C",), ("r", 0, 3, 3), ("C",), ("C",),
+    ("r", 0, 1, 1), ("ringend",), ("arel", 0), ("arel", 1), ("szs",), ("r", 1, 1, 2), ("r", 0, 1, 2),
+    ("szw",), ("syw",), ("aw",), ("C",), ("r", 1, 3, 0), ("r", 1, 1, 3), ("r", 0, 1, 3), ("C",),
+    ("r", 0, 3, 0), ("C",), ("C",), ("r", 0, 3, 1), ("r", 1, 3, 1), ("r", 1, 3, 2), ("r", 0, 3, 2), ("C",),
+    ("r", 1, 3, 3), ("C",), ("r", 0, 3, 3), ("E", 6), ("E", 7), ("C",), ("C",),
 )
 
 def rcopy(src, dst, send, recv, device):
@@ -55,9 +55,9 @@
 
 
 def kernel(
-    len_ref, a_hbm, g_hbm, out_ref, norm_ref,
-    a_ref, g_ref, gbuf, at, ats, gpack, gpair, gsum, gup, gdn, sup, sdn, sz, sy,
-    hold, own, s1, s2, s3, rl, rr, fl, fr,
+    len_hbm, a_hbm, g_hbm, out_ref, norm_ref,
+    len_ref, a_ref, g_ref, gbuf, at, ats, gpack, gpair, gsum, gup, gdn, sup, sdn, sz, sy,
+    hold, total, pre, own, s1, s2, s3, rl, rr, fl, fr,
     loads, ysend, yrecv, kup, kdn, zsend, zrecv, psend, precv, asend, a_near, a_other, a_far, afsend,
     gpsend, gprecv, gupsend, guprecv, gdnsend, gdnrecv, szsend, szrecv, sysend, syrecv,
     rsend, rlrecv, rrrecv, fsend, flrecv, frrecv,
@@ -87,6 +87,8 @@
 
     load_a = pltpu.make_async_copy(a_hbm, a_ref, loads.at[0])
     load_g = pltpu.make_async_copy(g_hbm, g_ref, loads.at[1])
+    load_len = pltpu.make_async_copy(len_hbm, len_ref, loads.at[2])
+    load_len.start()
     load_a.start()
     load_g.start()
 
@@ -97,6 +99,7 @@
         pl.semaphore_signal(barrier, inc=1, device_id=peer, device_id_type=pl.DeviceIdType.MESH)
     rows = lax.broadcasted_iota(jnp.int32, (SLOT_LEN, F), 0)
     contract = (((1,), (1,)), ((), ()))
+    load_len.wait()
     load_a.wait()
     load_g.wait()
 
@@ -218,7 +221,7 @@
             for k in range(Y):
                 factor = jnp.max(jnp.minimum(1.0, BOUND / jnp.sqrt(sy[ys(k) * 2 + h] + 1e-6)))
                 scaled = (at[ys(k), h].astype(F32) * factor).astype(BF16)
-                ats[:, pl.ds((h * Y + k) * SLOT_LEN, SLOT_LEN)] = scaled
+                ats[h, :, pl.ds(k * SLOT_LEN, SLOT_LEN)] = scaled
 
     def chunk(xb, j):
         return gbuf.at[xb, :, c, j] if j < 2 else gbuf.at[xb, j - 2, c, pl.ds(2, 2)]
@@ -289,25 +292,57 @@
             run_part(0, 128, 0)
             run_part(128, 128, 1)
 
+    def product(xb, q, core, slot, slots):
+        rows = gbuf[xb, q, core, pl.ds(slot, slots)].reshape(slots * SLOT_LEN, W)
+        cols = ats[core, :, pl.ds(slot * SLOT_LEN, slots * SLOT_LEN)]
+        return jnp.dot(cols, rows, preferred_element_type=F32)
+
+    def others(xb, j):
+        part = gbuf.at[xb, :, 1 - c, pl.ds(0, 2)] if j == 0 else gbuf.at[xb, j - 1, 1 - c, pl.ds(2, 2)]
+        wait_bytes(part, precv.at[xb, j])
+
+    def others_last(xb, q):
+        wait_bytes(gbuf.at[xb, q, 1 - c, pl.ds(2, 2)], precv.at[xb, 1 + q])
+
+    def ahead(t):
+        xb, q = info(t)
+        if t == 6:
+            @pl.when(is_src)
+            def _():
+                others(xb, 0)
+
+        pre[t - 6] = product(xb, q, c, 0, 2) + product(xb, q, 1 - c, 0, 2)
+
     def consume(t):
         xb, q = info(t)
 
-        @pl.when(q == 0)
-        def _():
-            wait_bytes(gbuf.at[xb, :, 1 - c, pl.ds(0, 2)], precv.at[xb, 0])
-
-        wait_bytes(gbuf.at[xb, q, 1 - c, pl.ds(2, 2)], precv.at[xb, 1 + q])
-        both = gbuf[xb, q].reshape(2 * Y * SLOT_LEN, W)
-        part = jnp.dot(ats[...], both, preferred_element_type=F32) * (1.0 / SEQS)
+        @pl.when(t < 6)
+        def _():
+            total[...] = product(xb, q, c, 0, 4)
+
+            @pl.when(q == 0)
+            def _():
+                others(xb, 0)
+
+            others_last(xb, q)
+            total[...] = (total[...] + product(xb, q, 1 - c, 0, 4)) * (1.0 / SEQS)
+
+        @pl.when(t >= 6)
+        def _():
+            late = lax.max(t - 6, 0)
+            total[...] = pre[late] + product(xb, q, c, 2, 2)
+            others_last(xb, q)
+            total[...] = (total[...] + product(xb, q, 1 - c, 2, 2)) * (1.0 / SEQS)
+
         o = lax.rem(xb + X - x, X)
 
         @pl.when(o == 0)
         def _():
-            own[q] = part
+            own[q] = total[...]
 
         @pl.when(o == 2)
         def _():
-            s2[q] = part.astype(BF16)
+            s2[q] = total[...].astype(BF16)
 
             def send(first, rows, slot):
                 relay_up(q, first, rows, slot).start()
@@ -317,15 +352,15 @@
 
         @pl.when(o == 1)
         def _():
-            s1[q, pl.ds(256, 256)] = part[256:].astype(BF16)
+            s1[q, pl.ds(256, 256)] = total[pl.ds(256, 256)].astype(BF16)
             final_up(q, 256, 256)
-            hold[lax.rem(t, 3)] = part[:256]
+            hold[lax.rem(t, 3)] = total[pl.ds(0, 256)]
 
         @pl.when(o == 3)
         def _():
-            s3[q, pl.ds(0, 256)] = part[:256].astype(BF16)
+            s3[q, pl.ds(0, 256)] = total[pl.ds(0, 256)].astype(BF16)
             final_dn(q, 0, 256)
-            hold[lax.rem(t, 3)] = part[256:]
+            hold[lax.rem(t, 3)] = total[pl.ds(256, 256)]
 
     def finish(t):
         xb, q = info(t)
@@ -353,7 +388,7 @@
             parts_of(t, add)
 
     calls = {
-        "gram": lambda: gram(1), "yl": first_steps, "yf": lambda q: first_far(3, q), "yg": lambda q: first_far(2, q), "o": own_chunk, "ol": own_left,
+        "gram": lambda: gram(1), "E": ahead, "yl": first_steps, "yf": lambda q: first_far(3, q), "yg": lambda q: first_far(2, q), "o": own_chunk, "ol": own_left,
         "pairs": pair.start, "pairw": pair_wait, "ring": ring, "ringend": ring_end, "szs": squares,
         "szw": squares_wait, "syw": norms_wait, "aw": scale, "acts": acts, "arel": act_relay,
     }
@@ -454,11 +489,12 @@
     dma, vmem = pltpu.SemaphoreType.DMA, pltpu.VMEM
     grams = (2, 3, 16, 128)
     scratch = [
+        pltpu.SMEM((2,), jnp.int32),
         vmem((2, SLOT_LEN, F), BF16),
         vmem((2, SLOT_LEN, F), BF16),
         vmem((X, NQ, 2, Y, SLOT_LEN, W), BF16),
         vmem((Y, 2, F, SLOT_LEN), BF16),
-        vmem((F, 2 * Y * SLOT_LEN), BF16),
+        vmem((2, F, Y * SLOT_LEN), BF16),
         vmem((2, Z) + grams, F32),
         vmem((Z,) + grams, F32),
         vmem((Z,) + grams, F32),
@@ -469,6 +505,8 @@
         vmem((Z, 8, 128), F32),
         vmem((2 * Y, 8, 128), F32),
         vmem((3, 256, W), F32),
+        vmem((F, W), F32),
+        vmem((2, F, W), F32),
         vmem((NQ, F, W), F32),
         vmem((NQ, F, W), BF16),
         vmem((NQ, F, W), BF16),
@@ -477,7 +515,7 @@
         vmem((NQ, 256, W), BF16),
         vmem((NQ, F, W), BF16),
         vmem((NQ, F, W), BF16),
-        dma((2,)), dma((NQ, 2)), dma((NQ, Y)), dma((4,)), dma((4,)), dma, dma((X, 4)),
+        dma((3,)), dma((NQ, 2)), dma((NQ, Y)), dma((4,)), dma((4,)), dma, dma((X, 4)),
         dma, dma((X, 3)), dma((2,)), dma((2,)), dma((2,)), dma((2,)), dma((2,)),
         dma, dma, dma((4,)), dma((4,)), dma((3,)), dma((3,)), dma, dma, dma, dma,
         dma((2,)), dma((NQ, 2)), dma((NQ, 2)), dma((2,)), dma((NQ,)), dma((NQ,)),
@@ -489,7 +527,7 @@
             jax.ShapeDtypeStruct((2,), F32),
         ),
         in_specs=[
-            pl.BlockSpec(memory_space=pltpu.SMEM),
+            pl.BlockSpec(memory_space=pl.ANY),
             pl.BlockSpec(memory_space=pl.ANY),
             pl.BlockSpec(memory_space=pl.ANY),
         ],

time: 85 us -> 85.8 us (level)
  Pallas kernels: 82.2 us -> 83.7 us
    pallas_call x1, Pallas kernels: 82.2 us -> 83.7 us  [local(): pl.pallas_call(kernel, out_shape=(jax.ShapeDtypeStruct((F, F), BF16), jax...]
where the time goes in v5:
time: 85.8 us; the launch traced here: 85.6 us
  Pallas kernels  83.7 us (98%)
  local copies, waits for them, and re-layouts  1.31 us (2%)
    pallas_call x1, Pallas kernels, local(): pl.pallas_call(kernel, out_shape=(jax.ShapeDtypeStruct((F, F), BF16), jax...  83.7 us

profile of v5, /device:TPU:4, one launch (start us, length us, event | category | flops | bytes accessed | tf_op | source)
XLA Modules:
  0.0 85.6 jit_solution(10847580217278194537)
XLA Ops:
  0.6 83.7 %shard_map.50 = (bf16[512,512]{1,0:T(8,128)(2,1)S(1)}, f32[2]{0:T(128)S(1)}) custom-call(s32[2]{0:T(128)} %len_hbm.1, bf16[2,256,512]{2,1,0:T(8,128)(2,1)} %a_hbm.1, bf16[2,256,512]{2,1,0:T(8,128)(2,1)} %g_hbm.1), custom_call_target="tpu_custom_call" | custom-call | flops 4294967296 | bytes 1572864 | tf_op jit(solution)/shard_map/pallas_call | solution.py:523
  84.3 0.8 copy.7
  85.1 0.5 copy.8

commit v6 on v5

--- a/solution.py
+++ b/solution.py
@@ -23,20 +23,20 @@
     ("yl",),
 )
 SOURCE = (
-    ("gram",), ("pairs",), ("o", 0), ("yf", 0), ("pairw",), ("yf", 1), ("yg", 0), ("ring", 1), ("acts", 1),
-    ("acts", 3), ("ring", 2), ("o", 1), ("ring", 3), ("o", 2), ("ring", 4), ("yg", 1), ("ringend",), ("szs",),
-    ("r", 1, 2, 0), ("r", 0, 2, 0), ("o", 3), ("arel", 0), ("arel", 1), ("szw",), ("r", 1, 2, 1), ("syw",),
-    ("aw",), ("r", 0, 2, 1), ("C",), ("r", 1, 2, 2), ("r", 0, 2, 2), ("C",), ("C",), ("C",), ("r", 1, 2, 3),
-    ("r", 0, 2, 3), ("r", 0, 4, 0), ("C",), ("C",), ("r", 1, 4, 1), ("r", 0, 4, 2), ("E", 6), ("C",),
-    ("E", 7), ("r", 1, 4, 3), ("C",),
+    ("yf", 0), ("gram",), ("pairs",), ("o", 0), ("pairw",), ("yf", 1), ("ring", 1), ("yg", 0), ("ring", 2),
+    ("o", 1), ("yg", 1), ("acts", 3), ("ring", 3), ("o", 2), ("ring", 4), ("acts", 1), ("ringend",),
+    ("arel", 1), ("szs",), ("r", 1, 2, 0), ("o", 3), ("arel", 0), ("r", 0, 2, 0), ("szw",), ("r", 1, 2, 1),
+    ("syw",), ("aw",), ("r", 0, 2, 1), ("r", 1, 2, 2), ("r", 0, 2, 2), ("C",), ("C",), ("C",), ("r", 1, 2, 3),
+    ("C",), ("r", 0, 2, 3), ("r", 0, 4, 0), ("C",), ("r", 1, 4, 1), ("C",), ("r", 0, 4, 2), ("E", 6),
+    ("E", 7), ("C",), ("r", 1, 4, 3), ("C",),
 )
 OTHER = (
-    ("yf", 0), ("gram",), ("pairs",), ("pairw",), ("ring", 1), ("yg", 0), ("ring", 2), ("acts", 3), ("yf", 1),
+    ("yf", 0), ("gram",), ("pairs",), ("pairw",), ("ring", 1), ("yf", 1), ("yg", 0), ("ring", 2), ("acts", 3),
     ("r", 0, 1, 0), ("yg", 1), ("ring", 3), ("r", 1, 1, 0), ("acts", 1), ("ring", 4), ("r", 1, 1, 1),
-    ("r", 0, 1, 1), ("ringend",), ("arel", 0), ("arel", 1), ("szs",), ("r", 1, 1, 2), ("r", 0, 1, 2),
-    ("szw",), ("syw",), ("aw",), ("C",), ("r", 1, 3, 0), ("r", 1, 1, 3), ("r", 0, 1, 3), ("C",),
-    ("r", 0, 3, 0), ("C",), ("C",), ("r", 0, 3, 1), ("r", 1, 3, 1), ("r", 1, 3, 2), ("r", 0, 3, 2), ("C",),
-    ("r", 1, 3, 3), ("C",), ("r", 0, 3, 3), ("E", 6), ("E", 7), ("C",), ("C",),
+    ("r", 0, 1, 1), ("arel", 0), ("ringend",), ("szs",), ("arel", 1), ("r", 1, 1, 2), ("r", 0, 1, 2),
+    ("szw",), ("syw",), ("aw",), ("C",), ("r", 1, 1, 3), ("r", 0, 1, 3), ("r", 0, 3, 0), ("r", 1, 3, 0),
+    ("C",), ("C",), ("C",), ("r", 1, 3, 1), ("r", 0, 3, 1), ("r", 1, 3, 2), ("r", 0, 3, 2), ("C",),
+    ("r", 1, 3, 3), ("C",), ("E", 6), ("r", 0, 3, 3), ("E", 7), ("C",), ("C",),
 )
 
 def rcopy(src, dst, send, recv, device):

time: 85.8 us -> 83.8 us (0.977)
  Pallas kernels: 83.7 us -> 81.7 us
    pallas_call x1, Pallas kernels: 83.7 us -> 81.7 us  [local(): pl.pallas_call(kernel, out_shape=(jax.ShapeDtypeStruct((F, F), BF16), jax...]
where the time goes in v6:
time: 83.8 us; the launch traced here: 83.6 us
  Pallas kernels  81.7 us (97%)
  local copies, waits for them, and re-layouts  1.31 us (2%)
    pallas_call x1, Pallas kernels, local(): pl.pallas_call(kernel, out_shape=(jax.ShapeDtypeStruct((F, F), BF16), jax...  81.7 us

profile of v6, /device:TPU:4, one launch (start us, length us, event | category | flops | bytes accessed | tf_op | source)
XLA Modules:
  0.0 83.6 jit_solution(15868664587652697464)
XLA Ops:
  0.6 81.7 %shard_map.50 = (bf16[512,512]{1,0:T(8,128)(2,1)S(1)}, f32[2]{0:T(128)S(1)}) custom-call(s32[2]{0:T(128)} %len_hbm.1, bf16[2,256,512]{2,1,0:T(8,128)(2,1)} %a_hbm.1, bf16[2,256,512]{2,1,0:T(8,128)(2,1)} %g_hbm.1), custom_call_target="tpu_custom_call" | custom-call | flops 4294967296 | bytes 1572864 | tf_op jit(solution)/shard_map/pallas_call | solution.py:523
  82.3 0.8 copy.7
  83.1 0.5 copy.8

commit v7 on v6

--- a/solution.py
+++ b/solution.py
@@ -23,20 +23,22 @@
     ("yl",),
 )
 SOURCE = (
-    ("yf", 0), ("gram",), ("pairs",), ("o", 0), ("pairw",), ("yf", 1), ("ring", 1), ("yg", 0), ("ring", 2),
-    ("o", 1), ("yg", 1), ("acts", 3), ("ring", 3), ("o", 2), ("ring", 4), ("acts", 1), ("ringend",),
+    ("yf", 0), ("gram",), ("pairs",), ("o", 0), ("pairw",), ("ring", 1), ("yf", 1), ("ring", 2), ("o", 1),
+    ("yg", 0), ("acts", 3), ("yg", 1), ("ring", 3), ("o", 2), ("ring", 4), ("acts", 1), ("ringend",),
     ("arel", 1), ("szs",), ("r", 1, 2, 0), ("o", 3), ("arel", 0), ("r", 0, 2, 0), ("szw",), ("r", 1, 2, 1),
-    ("syw",), ("aw",), ("r", 0, 2, 1), ("r", 1, 2, 2), ("r", 0, 2, 2), ("C",), ("C",), ("C",), ("r", 1, 2, 3),
-    ("C",), ("r", 0, 2, 3), ("r", 0, 4, 0), ("C",), ("r", 1, 4, 1), ("C",), ("r", 0, 4, 2), ("E", 6),
-    ("E", 7), ("C",), ("r", 1, 4, 3), ("C",),
+    ("syw",), ("aw",), ("r", 0, 2, 1), ("r", 1, 2, 2), ("r", 0, 2, 2), ("C",), ("C",), ("C",), ("F", 0),
+    ("r", 1, 2, 3), ("F", 1), ("C",), ("r", 0, 2, 3), ("r", 0, 4, 0), ("C",), ("F", 2), ("r", 1, 4, 1),
+    ("C",), ("F", 3), ("r", 0, 4, 2), ("E", 6), ("C",), ("F", 4), ("E", 7), ("F", 5), ("r", 1, 4, 3), ("C",),
+    ("F", 6), ("F", 7),
 )
 OTHER = (
     ("yf", 0), ("gram",), ("pairs",), ("pairw",), ("ring", 1), ("yf", 1), ("yg", 0), ("ring", 2), ("acts", 3),
     ("r", 0, 1, 0), ("yg", 1), ("ring", 3), ("r", 1, 1, 0), ("acts", 1), ("ring", 4), ("r", 1, 1, 1),
     ("r", 0, 1, 1), ("arel", 0), ("ringend",), ("szs",), ("arel", 1), ("r", 1, 1, 2), ("r", 0, 1, 2),
     ("szw",), ("syw",), ("aw",), ("C",), ("r", 1, 1, 3), ("r", 0, 1, 3), ("r", 0, 3, 0), ("r", 1, 3, 0),
-    ("C",), ("C",), ("C",), ("r", 1, 3, 1), ("r", 0, 3, 1), ("r", 1, 3, 2), ("r", 0, 3, 2), ("C",),
-    ("r", 1, 3, 3), ("C",), ("E", 6), ("r", 0, 3, 3), ("E", 7), ("C",), ("C",),
+    ("C",), ("C",), ("r", 1, 3, 1), ("F", 0), ("C",), ("F", 1), ("r", 0, 3, 1), ("r", 1, 3, 2),
+    ("r", 0, 3, 2), ("C",), ("F", 2), ("r", 1, 3, 3), ("C",), ("F", 3), ("E", 6), ("r", 0, 3, 3), ("E", 7),
+    ("C",), ("F", 4), ("C",), ("F", 5), ("F", 6), ("F", 7),
 )
 
 def rcopy(src, dst, send, recv, device):
@@ -283,6 +285,11 @@
         rcopy(s3.at[q, part], fr.at[q, part], fsend.at[1], frrecv.at[q], x_dn).start()
 
     def parts_of(t, run_part):
+        if isinstance(t, int):
+            for first, rows, slot in ((0, 128, 0), (128, 128, 1)) if t >= 6 else ((0, 256, 0),):
+                run_part(first, rows, slot)
+            return
+
         @pl.when(t < 6)
         def _():
             run_part(0, 256, 0)
@@ -365,7 +372,7 @@
     def finish(t):
         xb, q = info(t)
         o = lax.rem(xb + X - x, X)
-        s = lax.rem(t, 3)
+        s = t % 3
 
         @pl.when(o == 1)
         def _():
@@ -388,7 +395,7 @@
             parts_of(t, add)
 
     calls = {
-        "gram": lambda: gram(1), "E": ahead, "yl": first_steps, "yf": lambda q: first_far(3, q), "yg": lambda q: first_far(2, q), "o": own_chunk, "ol": own_left,
+        "gram": lambda: gram(1), "E": ahead, "F": finish, "yl": first_steps, "yf": lambda q: first_far(3, q), "yg": lambda q: first_far(2, q), "o": own_chunk, "ol": own_left,
         "pairs": pair.start, "pairw": pair_wait, "ring": ring, "ringend": ring_end, "szs": squares,
         "szw": squares_wait, "syw": norms_wait, "aw": scale, "acts": acts, "arel": act_relay,
     }
@@ -428,15 +435,14 @@
 
         consume(t)
 
-        @pl.when(t > 1)
-        def _():
-            finish(t - 2)
-
         return 0
 
     lax.fori_loop(0, 8, round_of, 0)
-    finish(6)
-    finish(7)
+    for src in (True, False):
+        @pl.when(is_src == src)
+        def _():
+            run(rounds[src][8])
+
 
     @pl.when(is_src)
     def _():

time: 83.8 us -> 84 us (level)
  no operation moved by 1% of the time
where the time goes in v7:
time: 84 us; the launch traced here: 83.6 us
  Pallas kernels  81.6 us (97%)
  local copies, waits for them, and re-layouts  1.31 us (2%)
    pallas_call x1, Pallas kernels, local(): pl.pallas_call(kernel, out_shape=(jax.ShapeDtypeStruct((F, F), BF16), jax...  81.6 us

profile of v7, /device:TPU:4, one launch (start us, length us, event | category | flops | bytes accessed | tf_op | source)
XLA Modules:
  0.0 83.6 jit_solution(12896155465407865623)
XLA Ops:
  0.6 81.6 %shard_map.50 = (bf16[512,512]{1,0:T(8,128)(2,1)S(1)}, f32[2]{0:T(128)S(1)}) custom-call(s32[2]{0:T(128)} %len_hbm.1, bf16[2,256,512]{2,1,0:T(8,128)(2,1)} %a_hbm.1, bf16[2,256,512]{2,1,0:T(8,128)(2,1)} %g_hbm.1), custom_call_target="tpu_custom_call" | custom-call | flops 4294967296 | bytes 1572864 | tf_op jit(solution)/shard_map/pallas_call | solution.py:529
  82.3 0.8 copy.7
  83.1 0.5 copy.8

commit v8 on v6

--- a/solution.py
+++ b/solution.py
@@ -20,18 +20,18 @@
 BF16 = jnp.bfloat16
 
 FIRST = (
-    ("yl",),
+    ("yl",), ("yf", 0), ("loaded",), ("gram0",),
 )
 SOURCE = (
-    ("yf", 0), ("gram",), ("pairs",), ("o", 0), ("pairw",), ("yf", 1), ("ring", 1), ("yg", 0), ("ring", 2),
-    ("o", 1), ("yg", 1), ("acts", 3), ("ring", 3), ("o", 2), ("ring", 4), ("acts", 1), ("ringend",),
-    ("arel", 1), ("szs",), ("r", 1, 2, 0), ("o", 3), ("arel", 0), ("r", 0, 2, 0), ("szw",), ("r", 1, 2, 1),
-    ("syw",), ("aw",), ("r", 0, 2, 1), ("r", 1, 2, 2), ("r", 0, 2, 2), ("C",), ("C",), ("C",), ("r", 1, 2, 3),
-    ("C",), ("r", 0, 2, 3), ("r", 0, 4, 0), ("C",), ("r", 1, 4, 1), ("C",), ("r", 0, 4, 2), ("E", 6),
-    ("E", 7), ("C",), ("r", 1, 4, 3), ("C",),
+    ("o", 0), ("gram",), ("pairs",), ("pairw",), ("yf", 1), ("ring", 1), ("yg", 0), ("ring", 2), ("o", 1),
+    ("yg", 1), ("acts", 3), ("ring", 3), ("o", 2), ("ring", 4), ("acts", 1), ("ringend",), ("arel", 1),
+    ("szs",), ("r", 1, 2, 0), ("o", 3), ("arel", 0), ("r", 0, 2, 0), ("szw",), ("r", 1, 2, 1), ("syw",),
+    ("aw",), ("r", 0, 2, 1), ("r", 1, 2, 2), ("r", 0, 2, 2), ("C",), ("C",), ("C",), ("r", 1, 2, 3), ("C",),
+    ("r", 0, 2, 3), ("r", 0, 4, 0), ("C",), ("r", 1, 4, 1), ("C",), ("r", 0, 4, 2), ("E", 6), ("E", 7),
+    ("C",), ("r", 1, 4, 3), ("C",),
 )
 OTHER = (
-    ("yf", 0), ("gram",), ("pairs",), ("pairw",), ("ring", 1), ("yf", 1), ("yg", 0), ("ring", 2), ("acts", 3),
+    ("gram",), ("pairs",), ("pairw",), ("ring", 1), ("yf", 1), ("yg", 0), ("ring", 2), ("acts", 3),
     ("r", 0, 1, 0), ("yg", 1), ("ring", 3), ("r", 1, 1, 0), ("acts", 1), ("ring", 4), ("r", 1, 1, 1),
     ("r", 0, 1, 1), ("arel", 0), ("ringend",), ("szs",), ("arel", 1), ("r", 1, 1, 2), ("r", 0, 1, 2),
     ("szw",), ("syw",), ("aw",), ("C",), ("r", 1, 1, 3), ("r", 0, 1, 3), ("r", 0, 3, 0), ("r", 1, 3, 0),
@@ -99,9 +99,11 @@
         pl.semaphore_signal(barrier, inc=1, device_id=peer, device_id_type=pl.DeviceIdType.MESH)
     rows = lax.broadcasted_iota(jnp.int32, (SLOT_LEN, F), 0)
     contract = (((1,), (1,)), ((), ()))
-    load_len.wait()
-    load_a.wait()
-    load_g.wait()
+
+    def loaded():
+        load_len.wait()
+        load_a.wait()
+        load_g.wait()
 
     def gram(s):
         am = jnp.where(rows < len_ref[s], a_ref[s].astype(F32), 0.0)
@@ -113,7 +115,6 @@
             gpack[s, :, m, 0] = full[:128, :128].reshape(Z, 16, 128)
             gpack[s, :, m, 1] = full[:128, 128:].reshape(Z, 16, 128)
             gpack[s, :, m, 2] = full[128:, 128:].reshape(Z, 16, 128)
-    gram(0)
     pl.semaphore_wait(barrier, len(peers))
 
     xb0 = lax.div(z, 2)
@@ -388,7 +389,7 @@
             parts_of(t, add)
 
     calls = {
-        "gram": lambda: gram(1), "E": ahead, "yl": first_steps, "yf": lambda q: first_far(3, q), "yg": lambda q: first_far(2, q), "o": own_chunk, "ol": own_left,
+        "loaded": loaded, "gram": lambda: gram(1), "gram0": lambda: gram(0), "E": ahead, "yl": first_steps, "yf": lambda q: first_far(3, q), "yg": lambda q: first_far(2, q), "o": own_chunk, "ol": own_left,
         "pairs": pair.start, "pairw": pair_wait, "ring": ring, "ringend": ring_end, "szs": squares,
         "szw": squares_wait, "syw": norms_wait, "aw": scale, "acts": acts, "arel": act_relay,
     }

time: 83.8 us -> 83.7 us (level)
  no operation moved by 1% of the time
where the time goes in v8:
time: 83.7 us; the launch traced here: 83.6 us
  Pallas kernels  81.7 us (98%)
  local copies, waits for them, and re-layouts  1.31 us (2%)
    pallas_call x1, Pallas kernels, local(): pl.pallas_call(kernel, out_shape=(jax.ShapeDtypeStruct((F, F), BF16), jax...  81.7 us

profile of v8, /device:TPU:4, one launch (start us, length us, event | category | flops | bytes accessed | tf_op | source)
XLA Modules:
  0.0 83.6 jit_solution(10801753649255456196)
XLA Ops:
  0.6 81.7 %shard_map.50 = (bf16[512,512]{1,0:T(8,128)(2,1)S(1)}, f32[2]{0:T(128)S(1)}) custom-call(s32[2]{0:T(128)} %len_hbm.1, bf16[2,256,512]{2,1,0:T(8,128)(2,1)} %a_hbm.1, bf16[2,256,512]{2,1,0:T(8,128)(2,1)} %g_hbm.1), custom_call_target="tpu_custom_call" | custom-call | flops 4294967296 | bytes 1572864 | tf_op jit(solution)/shard_map/pallas_call | solution.py:524
  82.3 0.8 copy.7
  83.1 0.5 copy.8

commit v9 on v8

--- a/solution.py
+++ b/solution.py
@@ -23,16 +23,16 @@
     ("yl",), ("yf", 0), ("loaded",), ("gram0",),
 )
 SOURCE = (
-    ("o", 0), ("gram",), ("pairs",), ("pairw",), ("yf", 1), ("ring", 1), ("yg", 0), ("ring", 2), ("o", 1),
+    ("yf", 1), ("o", 0), ("gram",), ("pairs",), ("pairw",), ("ring", 1), ("yg", 0), ("ring", 2), ("o", 1),
     ("yg", 1), ("acts", 3), ("ring", 3), ("o", 2), ("ring", 4), ("acts", 1), ("ringend",), ("arel", 1),
     ("szs",), ("r", 1, 2, 0), ("o", 3), ("arel", 0), ("r", 0, 2, 0), ("szw",), ("r", 1, 2, 1), ("syw",),
-    ("aw",), ("r", 0, 2, 1), ("r", 1, 2, 2), ("r", 0, 2, 2), ("C",), ("C",), ("C",), ("r", 1, 2, 3), ("C",),
+    ("aw",), ("r", 0, 2, 1), ("r", 0, 2, 2), ("C",), ("r", 1, 2, 2), ("C",), ("C",), ("r", 1, 2, 3), ("C",),
     ("r", 0, 2, 3), ("r", 0, 4, 0), ("C",), ("r", 1, 4, 1), ("C",), ("r", 0, 4, 2), ("E", 6), ("E", 7),
     ("C",), ("r", 1, 4, 3), ("C",),
 )
 OTHER = (
     ("gram",), ("pairs",), ("pairw",), ("ring", 1), ("yf", 1), ("yg", 0), ("ring", 2), ("acts", 3),
-    ("r", 0, 1, 0), ("yg", 1), ("ring", 3), ("r", 1, 1, 0), ("acts", 1), ("ring", 4), ("r", 1, 1, 1),
+    ("r", 0, 1, 0), ("yg", 1), ("ring", 3), ("r", 1, 1, 0), ("ring", 4), ("acts", 1), ("r", 1, 1, 1),
     ("r", 0, 1, 1), ("arel", 0), ("ringend",), ("szs",), ("arel", 1), ("r", 1, 1, 2), ("r", 0, 1, 2),
     ("szw",), ("syw",), ("aw",), ("C",), ("r", 1, 1, 3), ("r", 0, 1, 3), ("r", 0, 3, 0), ("r", 1, 3, 0),
     ("C",), ("C",), ("C",), ("r", 1, 3, 1), ("r", 0, 3, 1), ("r", 1, 3, 2), ("r", 0, 3, 2), ("C",),

time: 83.7 us -> 83.8 us (level)
  no operation moved by 1% of the time
where the time goes in v9:
time: 83.8 us; the launch traced here: 83.7 us
  Pallas kernels  81.7 us (97%)
  local copies, waits for them, and re-layouts  1.31 us (2%)
    pallas_call x1, Pallas kernels, local(): pl.pallas_call(kernel, out_shape=(jax.ShapeDtypeStruct((F, F), BF16), jax...  81.7 us

profile of v9, /device:TPU:4, one launch (start us, length us, event | category | flops | bytes accessed | tf_op | source)
XLA Modules:
  0.0 83.7 jit_solution(10440290794045870592)
XLA Ops:
  0.6 81.7 %shard_map.50 = (bf16[512,512]{1,0:T(8,128)(2,1)S(1)}, f32[2]{0:T(128)S(1)}) custom-call(s32[2]{0:T(128)} %len_hbm.1, bf16[2,256,512]{2,1,0:T(8,128)(2,1)} %a_hbm.1, bf16[2,256,512]{2,1,0:T(8,128)(2,1)} %g_hbm.1), custom_call_target="tpu_custom_call" | custom-call | flops 4294967296 | bytes 1572864 | tf_op jit(solution)/shard_map/pallas_call | solution.py:524
  82.4 0.8 copy.7
  83.1 0.5 copy.8
